TPU v7x, 256 devices: a whole 4x4x8 slice. The times are simulated.
256 devices in a mesh: cpx: 16 (over y, z_lo, core), cpy: 16 (over x, z_hi).
Axes of the slice: x: 4, y: 4, z: 8 (z_hi: 4, z_lo: 2; z = z_hi * 2 + z_lo), core: 2. Of those that a mesh axis runs over, the one named last changes fastest.
Arguments:
- queries: bfloat16 [49152, 1024], P(('cpx', 'cpy')), may hold values from -6 to 6
- grad_out: bfloat16 [49152, 1024], P(('cpx', 'cpy')), may hold values from -60 to 60
- attn_out: bfloat16 [49152, 1024], P(('cpx', 'cpy')), may hold values from -6 to 6
- saved_lse: float32 [8, 49152], P(None, ('cpx', 'cpy')), may hold values from 6 to 8
- key_rows: bfloat16 [196608, 128], P(('cpx', 'cpy')), may hold values from -6 to 6
- value_rows: bfloat16 [196608, 128], P(('cpx', 'cpy')), may hold values from -6 to 6
- doc_lengths: int32 [64], replicated, may hold values from 1 to 6144, 196608 in all
- read_steps: int32 [256, 4], replicated, may hold values from -1 to 255, as said below
Outputs:
- grad_queries: float32 [49152, 1024], P(('cpx', 'cpy'))
- grad_keys: float32 [196608, 128], P(('cpx', 'cpy'))
- grad_values: float32 [196608, 128], P(('cpx', 'cpy'))
Inputs may be any that keep to these rules, and one draw needn't show every extreme that they name: `read_steps`: entry (d, t) is d - t if device d reads the key block of device d - t and -1 if not; entry (d, 0) is d; entries with d - t < 0 are -1.
All inputs are finite; a program needn't handle non-finite values.
Results may differ from a plain program's by a relative error of at most 0.0044.
Values may be sent and summed in bfloat16 or wider, within the bound.
No kernel may reach another device: no remote copies, remote signals or barrier semaphores. Data moves between devices by JAX's collectives and lax.ppermute only.
A program may use at most 64 MiB of HBM per device.

v0:
```python
import jax
import jax.numpy as jnp
from jax import lax
from jax.sharding import PartitionSpec as P

STEPS = 4


def passed_along(value, axis, steps):
    count = lax.axis_size(axis)
    leading, last = (max(0, -steps), min(count, count - steps))
    return lax.ppermute(value, axis, [(source, source + steps) for source in range(leading, last)])


def doc_index(positions, doc_ends):
    return jnp.sum((doc_ends[None, :] <= positions[:, None]).astype(jnp.int32), axis=1)


def pair_grads(pair_rows, saved_stats, own_block, allowed, active):
    row_count = pair_rows.shape[1]
    head_dim = own_block.shape[2]
    block_len = own_block.shape[1]
    head_count = pair_rows.shape[2] // head_dim
    score_scale = head_dim ** (-0.5)
    contract_last = (((1,), (1,)), ((), ()))
    contract_first = (((0,), (0,)), ((), ()))

    def compute():
        query_flat = pair_rows[0].reshape(row_count * head_count, head_dim)
        grad_flat = pair_rows[1].reshape(row_count * head_count, head_dim)
        lse_rows = saved_stats[0].T.reshape(row_count, head_count, 1)
        delta_rows = saved_stats[1].T.reshape(-1)
        scores = (
            lax.dot_general(
                query_flat, own_block[0], contract_last, preferred_element_type=jnp.float32
            )
            * score_scale
        )
        shaped = scores.reshape(row_count, head_count, block_len)
        weights = jnp.where(allowed[:, None, :], jnp.exp(shaped - lse_rows), 0.0).reshape(
            row_count * head_count, block_len
        )
        grad_weights = lax.dot_general(
            grad_flat, own_block[1], contract_last, preferred_element_type=jnp.float32
        )
        grad_scores = weights * (grad_weights - delta_rows[:, None])
        weight_half = weights.astype(jnp.bfloat16)
        score_half = grad_scores.astype(jnp.bfloat16)
        grad_query = (
            jnp.dot(score_half, own_block[0], preferred_element_type=jnp.float32) * score_scale
        )
        grad_key = (
            lax.dot_general(
                score_half, query_flat, contract_first, preferred_element_type=jnp.float32
            )
            * score_scale
        )
        grad_value = lax.dot_general(
            weight_half, grad_flat, contract_first, preferred_element_type=jnp.float32
        )
        return (
            grad_query.reshape(row_count, head_count * head_dim),
            jnp.stack([grad_key, grad_value]),
        )

    def nothing():
        return (
            jnp.zeros((row_count, head_count * head_dim), jnp.float32),
            jnp.zeros((2, block_len, head_dim), jnp.float32),
        )

    return lax.cond(active, compute, nothing)


def spread(payload, direction, sender):
    result = [payload]
    for distance in range(1, STEPS):
        result.append(sender(payload, direction * distance))
    return result


def collect(partials, direction, sender):
    summed = partials[0]
    for distance in range(1, STEPS):
        summed = summed + sender(partials[distance], -direction * distance)
    return summed


def send_keys(payload, offset):
    return passed_along(payload, ("cpx", "cpy"), offset)


def send_grads(payload, offset):
    return passed_along(payload, ("cpx", "cpy"), offset)


def local(queries, grad_out, attn_out, saved_lse, key_rows, value_rows, doc_lengths, read_steps):
    row_count, row_width = queries.shape
    block_len, head_dim = key_rows.shape
    head_count = row_width // head_dim
    device_count = lax.axis_size(("cpx", "cpy"))
    device = lax.axis_index(("cpx", "cpy"))
    doc_ends = jnp.cumsum(doc_lengths, dtype=jnp.int32)
    row_delta = jnp.sum(
        grad_out.astype(jnp.float32).reshape(row_count, head_count, head_dim)
        * attn_out.astype(jnp.float32).reshape(row_count, head_count, head_dim),
        axis=2,
    )
    saved_stats = jnp.stack([saved_lse, row_delta.T])
    pair_rows = jnp.stack([queries, grad_out])
    own_block = jnp.stack([key_rows, value_rows])
    query_iota = jnp.arange(row_count, dtype=jnp.int32)
    key_iota = jnp.arange(block_len, dtype=jnp.int32)
    blocks = spread(own_block, 1, send_keys)
    partials = []
    query_total = None
    for distance in range(STEPS):
        owner_id = device - distance
        query_pos = device * block_len + (block_len - row_count) + query_iota
        key_pos = owner_id * block_len + key_iota
        allowed = (
            doc_index(query_pos, doc_ends)[:, None] == doc_index(key_pos, doc_ends)[None, :]
        ) & (key_pos[None, :] <= query_pos[:, None])
        safe_reader = jnp.clip(device, 0, device_count - 1)
        active = (
            (owner_id >= 0)
            & (device < device_count)
            & (read_steps[safe_reader, distance] == owner_id)
        )
        allowed, active = (allowed, active)
        grad_query, grad_pair = pair_grads(
            pair_rows, saved_stats, blocks[distance], allowed, active
        )
        query_total = grad_query if distance == 0 else query_total + grad_query
        partials.append(grad_pair)
    pair_total = collect(partials, 1, send_grads)
    return (query_total, pair_total[0], pair_total[1])


def solution(mesh):
    return jax.shard_map(
        local,
        mesh=mesh,
        in_specs=(
            P(("cpx", "cpy"), None),
            P(("cpx", "cpy"), None),
            P(("cpx", "cpy"), None),
            P(None, ("cpx", "cpy")),
            P(("cpx", "cpy"), None),
            P(("cpx", "cpy"), None),
            P(),
            P(),
        ),
        out_specs=(P(("cpx", "cpy"), None), P(("cpx", "cpy"), None), P(("cpx", "cpy"), None)),
        check_vma=False,
    )
```

profile of v0, /device:TPU:173, one launch (start us, length us, event | category | flops | bytes accessed | tf_op | source)
XLA Modules:
  0.0 144.9 jit_solution(10462460708569831667)
XLA Ops:
  0.7 1.9 %pad_maximum_fusion.4 = bf16[2,768,128]{2,1,0:T(8,128)(2,1)} fusion(bf16[1,768,128]{2,1,0:T(8,128)(2,1)} %bitcast.103, bf16[1,768,128]{2,1,0:T(8,128)(2,1)} %bitcast.102), kind=kLoop, calls=%fused_computation.63 | loop fusion | flops 196608 | bytes 786432 | tf_op jit(solution)/shard_map/stack | solution.py:111
  2.5 3.1 %collective-permute-start = (bf16[2,768,128]{2,1,0:T(8,128)(2,1)}, bf16[2,768,128]{2,1,0:T(8,128)(2,1)S(1)}, u32[]{:S(2)}, u32[]{:S(2)}) collective-permute-start(bf16[2,768,128]{2,1,0:T(8,128)(2,1)} %pad_maximum_fusion.4), channel_id=1, source_target_pairs={{0,1},{1,2},{2,3},{3,4},{4,5},{5,6},{6,7},{7,8},{8,9},{9,10},{10,1... | collective-permute-start | bytes 1179656 | tf_op jit(solution)/shard_map/ppermute | solution.py:12
  5.6 3.7 %collective-permute-start.1 = (bf16[2,768,128]{2,1,0:T(8,128)(2,1)}, bf16[2,768,128]{2,1,0:T(8,128)(2,1)}, u32[]{:S(2)}, u32[]{:S(2)}) collective-permute-start(bf16[2,768,128]{2,1,0:T(8,128)(2,1)} %pad_maximum_fusion.4), channel_id=1, source_target_pairs={{0,2},{1,3},{2,4},{3,5},{4,6},{5,7},{6,8},{7,9},{8,10},{9,11},{10,... | collective-permute-start | bytes 1179656 | tf_op jit(solution)/shard_map/ppermute | solution.py:12
  9.3 4.1 %collective-permute-start.2 = (bf16[2,768,128]{2,1,0:T(8,128)(2,1)}, bf16[2,768,128]{2,1,0:T(8,128)(2,1)}, u32[]{:S(2)}, u32[]{:S(2)}) collective-permute-start(bf16[2,768,128]{2,1,0:T(8,128)(2,1)} %pad_maximum_fusion.4), channel_id=1, source_target_pairs={{0,3},{1,4},{2,5},{3,6},{4,7},{5,8},{6,9},{7,10},{8,11},{9,12},{10... | collective-permute-start | bytes 1179656 | tf_op jit(solution)/shard_map/ppermute | solution.py:12
  13.5 1.2 multiply_bitcast_fusion
  14.7 0.7 copy.17
  15.6 0.1 reduce
  15.7 0.1 copy.22
  15.8 1.5 %constant_dynamic-slice_fusion.2 = (s32[1,1]{0,1:T(1,128)}, s32[1,1]{0,1:T(1,128)}, s32[1,1]{0,1:T(1,128)}, s32[1,1]{0,1:T(1,128)}) fusion(s32[256,4]{0,1:T(4,128)} %param.23, s32[]{:T(128)S(6)} %min.7), kind=kLoop, calls=%fused_computation.76 | loop fusion | bytes 36 | tf_op jit(solution)/shard_map/dynamic_slice | solution.py:128
  19.3 0.3 reduce_sum.56
  19.7 1.5 %compare_convert_fusion.2 = (s32[768,64]{1,0:T(8,128)S(1)}, s32[768,64]{1,0:T(8,128)}, s32[768,64]{1,0:T(8,128)}, s32[768,64]{1,0:T(8,128)}) fusion(s32[64]{0:T(128)S(1)} %reduce, s32[768]{0:T(1024)S(1)} %iota_add_fusion.2, s32[768]{0:T(1024)S(1)} %iota_add_fusion.1, s32[768]{0:T(1024)S(1)} %iota_add_fusion, s32[768]{0:T(1024)S(1)} %iota_add_fusion.3), kind=kLoop, calls=%fused_computation.66 | loop fusion | flops 393216 | bytes 798976 | tf_op jit(solution)/shard_map/convert_element_type | solution.py:16
  21.1 12.5 %collective-permute-done = bf16[2,768,128]{2,1,0:T(8,128)(2,1)S(1)} collective-permute-done((bf16[2,768,128]{2,1,0:T(8,128)(2,1)}, bf16[2,768,128]{2,1,0:T(8,128)(2,1)S(1)}, u32[]{:S(2)}, u32[]{:S(2)}) %collective-permute-start) | collective-permute-done | bytes 393248 | tf_op jit(solution)/shard_map/ppermute | solution.py:12
  33.7 0.7 copy-done.4
  34.7 13.4 %conditional.5 = (f32[192,1024]{1,0:T(8,128)}, f32[2,768,128]{2,1,0:T(8,128)}) conditional(s32[]{:T(128)} %convert_element_type.65, () %tuple.42, (s32[192,768]{1,0:T(8,128)S(1)}, bf16[192,1024]{1,0:T(8,128)(2,1)S(1)}, bf16[2,768,128]{2,1,0:T(8,128)(2,1)}, f32[8,192]{1,0:T(8,128)S(1)}, bf16[192,1024]{1,0:T(8,128)(2,1)S(1)}, ...), branch_computations={%region_7.8_spmd, %region_8.9_spmd} | conditional | flops 1519189248 | bytes 47146080 | solution.py:72
  34.7 0.2 squeeze_stack.18
  34.9 0.2 reduce_sum.73
  35.0 0.1 compare_and_fusion.1
  35.2 0.1 copy.19
  35.3 0.1 sub.72
  35.4 4.4 %exponential_select_fusion.1 = f32[1536,768]{1,0:T(8,128)} fusion(bf16[1536,128]{1,0:T(8,128)(2,1)S(1)} %squeeze_stack.18, f32[1536]{0:T(1024)S(1)} %sub.72, pred[192,768]{1,0:T(8,128)(4,1)S(1)} %compare_and_fusion.1, bf16[2,768,128]{2,1,0:T(8,128)(2,1)} %get-tuple-element.59), kind=kOutput, calls=%fused_computation.11 | convolution fusion | flops 305528832 | bytes 5462016 | tf_op jit(solution)/shard_map/cond/branch_1_fun/dot_general | solution.py:34
  39.8 0.2 squeeze_stack.19
  40.1 3.4 %multiply_convert_fusion.1 = bf16[1536,768]{1,0:T(8,128)(2,1)S(1)} fusion(f32[1536,768]{1,0:T(8,128)} %exponential_select_fusion.1, bf16[1536,128]{1,0:T(8,128)(2,1)S(1)} %squeeze_stack.19, f32[1536]{0:T(1024)S(1)} %sub.75, bf16[2,768,128]{2,1,0:T(8,128)(2,1)} %get-tuple-element.59), kind=kOutput, calls=%fused_computation.10 | convolution fusion | flops 305528832 | bytes 7673856 | tf_op jit(solution)/shard_map/cond/branch_1_fun/dot_general | solution.py:43
  43.5 0.8 fusion.11
  44.4 0.8 fusion.8
  45.2 1.1 pad_maximum_fusion.1
  46.2 0.8 convolution_multiply_fusion.2
  47.0 1.0 reshape.121
  48.0 3.2 %collective-permute-start.3 = (f32[2,768,128]{2,1,0:T(8,128)}, f32[2,768,128]{2,1,0:T(8,128)}, u32[]{:S(2)}, u32[]{:S(2)}) collective-permute-start(f32[2,768,128]{2,1,0:T(8,128)} %get-tuple-element.91), channel_id=1, source_target_pairs={{1,0},{2,1},{3,2},{4,3},{5,4},{6,5},{7,6},{8,7},{9,8},{10,9},{11,1... | collective-permute-start | bytes 2359304 | tf_op jit(solution)/shard_map/ppermute | solution.py:12
  51.3 15.5 %conditional.6 = (f32[192,1024]{1,0:T(8,128)}, f32[2,768,128]{2,1,0:T(8,128)}) conditional(s32[]{:T(128)} %convert_element_type.67, () %tuple.44, (s32[192,768]{1,0:T(8,128)S(1)}, bf16[192,1024]{1,0:T(8,128)(2,1)S(1)}, bf16[2,768,128]{2,1,0:T(8,128)(2,1)}, f32[8,192]{1,0:T(8,128)S(1)}, bf16[192,1024]{1,0:T(8,128)(2,1)S(1)}, ...), branch_computations={%region_10.11_spmd, %region_11.12_spmd} | conditional | flops 1519189248 | bytes 45573188 | solution.py:72
  51.5 0.2 squeeze_stack.20
  51.7 1.2 reduce_sum.74
  52.8 0.1 compare_and_fusion.2
  53.1 0.1 sub.78
  53.2 4.4 %exponential_select_fusion.2 = f32[1536,768]{1,0:T(8,128)} fusion(bf16[1536,128]{1,0:T(8,128)(2,1)S(1)} %squeeze_stack.20, f32[1536]{0:T(1024)S(1)} %sub.78, pred[192,768]{1,0:T(8,128)(4,1)S(1)} %compare_and_fusion.2, bf16[2,768,128]{2,1,0:T(8,128)(2,1)} %get-tuple-element.65), kind=kOutput, calls=%fused_computation.27 | convolution fusion | flops 305528832 | bytes 5462016 | tf_op jit(solution)/shard_map/cond/branch_1_fun/dot_general | solution.py:34
  57.6 0.2 squeeze_stack.21
  57.9 3.4 %multiply_convert_fusion.2 = bf16[1536,768]{1,0:T(8,128)(2,1)S(1)} fusion(f32[1536,768]{1,0:T(8,128)} %exponential_select_fusion.2, bf16[1536,128]{1,0:T(8,128)(2,1)S(1)} %squeeze_stack.21, f32[1536]{0:T(1024)S(1)} %sub.81, bf16[2,768,128]{2,1,0:T(8,128)(2,1)} %get-tuple-element.65), kind=kOutput, calls=%fused_computation.26 | convolution fusion | flops 305528832 | bytes 7673856 | tf_op jit(solution)/shard_map/cond/branch_1_fun/dot_general | solution.py:43
  61.3 0.8 fusion.23
  62.1 0.8 fusion.20
  62.9 1.0 pad_maximum_fusion.2
  63.9 1.7 %convolution_multiply_fusion.4 = f32[1536,128]{1,0:T(8,128)S(1)} fusion(bf16[1536,768]{1,0:T(8,128)(2,1)S(1)} %multiply_convert_fusion.2, bf16[2,768,128]{2,1,0:T(8,128)(2,1)} %get-tuple-element.65), kind=kOutput, calls=%fused_computation.28 | convolution fusion | flops 302186496 | bytes 3342336 | tf_op jit(solution)/shard_map/cond/branch_1_fun/dot_general | solution.py:50
  65.7 1.1 reshape.122
  66.7 4.1 %collective-permute-start.4 = (f32[2,768,128]{2,1,0:T(8,128)}, f32[2,768,128]{2,1,0:T(8,128)}, u32[]{:S(2)}, u32[]{:S(2)}) collective-permute-start(f32[2,768,128]{2,1,0:T(8,128)} %get-tuple-element.92), channel_id=1, source_target_pairs={{2,0},{3,1},{4,2},{5,3},{6,4},{7,5},{8,6},{9,7},{10,8},{11,9},{12,... | collective-permute-start | bytes 2359304 | tf_op jit(solution)/shard_map/ppermute | solution.py:12
  70.8 1.9 %conditional.7 = (f32[192,1024]{1,0:T(8,128)}, f32[2,768,128]{2,1,0:T(8,128)}) conditional(s32[]{:T(128)} %convert_element_type.69, () %tuple.46, (s32[192,768]{1,0:T(8,128)S(1)}, bf16[192,1024]{1,0:T(8,128)(2,1)S(1)}, bf16[2,768,128]{2,1,0:T(8,128)(2,1)}, f32[8,192]{1,0:T(8,128)S(1)}, bf16[192,1024]{1,0:T(8,128)(2,1)S(1)}, ...), branch_computations={%region_13.14_spmd, %region_14.15_spmd} | conditional | flops 1519189248 | bytes 45573188 | solution.py:72
  70.8 1.0 broadcast.112
  71.8 0.9 broadcast.113
  72.7 17.5 %collective-permute-start.5 = (f32[2,768,128]{2,1,0:T(8,128)}, f32[2,768,128]{2,1,0:T(8,128)}, u32[]{:S(2)}, u32[]{:S(2)}) collective-permute-start(f32[2,768,128]{2,1,0:T(8,128)} %get-tuple-element.93), channel_id=1, source_target_pairs={{3,0},{4,1},{5,2},{6,3},{7,4},{8,5},{9,6},{10,7},{11,8},{12,9},{13... | collective-permute-start | bytes 2359304 | tf_op jit(solution)/shard_map/ppermute | solution.py:12
  90.9 13.5 %conditional.4 = (f32[192,1024]{1,0:T(8,128)S(1)}, f32[2,768,128]{2,1,0:T(8,128)}) conditional(s32[]{:T(128)} %convert_element_type.60, () %tuple.40, (s32[192,768]{1,0:T(8,128)S(1)}, bf16[192,1024]{1,0:T(8,128)(2,1)S(1)}, bf16[768,128]{1,0:T(8,128)(2,1)}, f32[8,192]{1,0:T(8,128)S(1)}, bf16[192,1024]{1,0:T(8,128)(2,1)S(1)}, ...), branch_computations={%region_4.5_spmd, %region_5.6_spmd} | conditional | flops 1519189248 | bytes 47146108 | solution.py:72
  91.2 0.2 squeeze_stack.16
  91.4 1.2 reduce_sum.72
  92.5 0.1 compare_and_fusion
  92.8 0.1 sub.55
  92.9 4.4 %exponential_select_fusion = f32[1536,768]{1,0:T(8,128)} fusion(bf16[1536,128]{1,0:T(8,128)(2,1)S(1)} %squeeze_stack.16, bf16[768,128]{1,0:T(8,128)(2,1)} %get-tuple-element.52, f32[1536]{0:T(1024)S(1)} %sub.55, pred[192,768]{1,0:T(8,128)(4,1)S(1)} %compare_and_fusion), kind=kOutput, calls=%fused_computation.1 | convolution fusion | flops 305528832 | bytes 5462016 | tf_op jit(solution)/shard_map/cond/branch_1_fun/dot_general | solution.py:34
  97.3 0.2 squeeze_stack.17
  97.6 3.3 %multiply_convert_fusion = bf16[1536,768]{1,0:T(8,128)(2,1)S(1)} fusion(f32[1536,768]{1,0:T(8,128)} %exponential_select_fusion, bf16[1536,128]{1,0:T(8,128)(2,1)S(1)} %squeeze_stack.17, bf16[768,128]{1,0:T(8,128)(2,1)S(1)} %copy-done.3, f32[1536]{0:T(1024)S(1)} %sub.58), kind=kOutput, calls=%fused_computation | convolution fusion | flops 305528832 | bytes 7673856 | tf_op jit(solution)/shard_map/cond/branch_1_fun/dot_general | solution.py:43
  100.9 0.8 fusion.5
  101.8 0.8 fusion.2
  102.6 1.0 pad_maximum_fusion
  103.6 0.8 convolution_multiply_fusion
  104.4 0.1 reshape.120
  104.5 2.8 %add_add_fusion.1 = f32[192,1024]{1,0:T(8,128)} fusion(f32[192,1024]{1,0:T(8,128)} %get-tuple-element.89, f32[192,1024]{1,0:T(8,128)} %get-tuple-element.88, f32[192,1024]{1,0:T(8,128)S(1)} %get-tuple-element.86, f32[192,1024]{1,0:T(8,128)} %get-tuple-element.87), kind=kLoop, calls=%fused_computation.59 | loop fusion | flops 589824 | bytes 3932160 | tf_op jit(solution)/shard_map/add | solution.py:134
  107.3 13.3 %collective-permute-done.4 = f32[2,768,128]{2,1,0:T(8,128)} collective-permute-done((f32[2,768,128]{2,1,0:T(8,128)}, f32[2,768,128]{2,1,0:T(8,128)}, u32[]{:S(2)}, u32[]{:S(2)}) %collective-permute-start.4) | collective-permute-done | bytes 786464 | tf_op jit(solution)/shard_map/ppermute | solution.py:12
  120.6 21.4 %collective-permute-done.5 = f32[2,768,128]{2,1,0:T(8,128)} collective-permute-done((f32[2,768,128]{2,1,0:T(8,128)}, f32[2,768,128]{2,1,0:T(8,128)}, u32[]{:S(2)}, u32[]{:S(2)}) %collective-permute-start.5) | collective-permute-done | bytes 786464 | tf_op jit(solution)/shard_map/ppermute | solution.py:12
  142.0 2.0 %add_add_fusion = f32[2,768,128]{2,1,0:T(8,128)S(1)} fusion(f32[2,768,128]{2,1,0:T(8,128)} %collective-permute-done.5, f32[2,768,128]{2,1,0:T(8,128)} %collective-permute-done.4, f32[2,768,128]{2,1,0:T(8,128)} %get-tuple-element.90, f32[2,768,128]{2,1,0:T(8,128)} %collective-permute-done.3), kind=kLoop, calls=%fused_computation.58 | loop fusion | flops 589824 | bytes 3932160 | tf_op jit(solution)/shard_map/add | solution.py:85
  144.0 0.9 slice_bitcast_fusion
  (45 shorter events, 1.0 us)
Async XLA Ops:
  0.6 34.0 %copy-start = (bf16[192,1024]{1,0:T(8,128)(2,1)S(1)}, bf16[192,1024]{1,0:T(8,128)(2,1)}, u32[]{:S(2)}) copy-start(bf16[192,1024]{1,0:T(8,128)(2,1)} %param.17) | copy-start | bytes 1179652
  0.6 34.0 %copy-start.1 = (bf16[192,1024]{1,0:T(8,128)(2,1)S(1)}, bf16[192,1024]{1,0:T(8,128)(2,1)}, u32[]{:S(2)}) copy-start(bf16[192,1024]{1,0:T(8,128)(2,1)} %param.16) | copy-start | bytes 1179652
  0.7 34.0 %copy-start.6 = (f32[8,192]{1,0:T(8,128)S(1)}, f32[8,192]{1,0:T(8,128)}, u32[]{:S(2)}) copy-start(f32[8,192]{1,0:T(8,128)} %param.19) | copy-start | bytes 18436
  2.5 31.1 %collective-permute-start = (bf16[2,768,128]{2,1,0:T(8,128)(2,1)}, bf16[2,768,128]{2,1,0:T(8,128)(2,1)S(1)}, u32[]{:S(2)}, u32[]{:S(2)}) collective-permute-start(bf16[2,768,128]{2,1,0:T(8,128)(2,1)} %pad_maximum_fusion.4), channel_id=1, source_target_pairs={{0,1},{1,2},{2,3},{3,4},{4,5},{5,6},{6,7},{7,8},{8,9},{9,10},{10,1... | collective-permute-start | bytes 1179656 | tf_op jit(solution)/shard_map/ppermute | solution.py:12
  5.6 45.6 %collective-permute-start.1 = (bf16[2,768,128]{2,1,0:T(8,128)(2,1)}, bf16[2,768,128]{2,1,0:T(8,128)(2,1)}, u32[]{:S(2)}, u32[]{:S(2)}) collective-permute-start(bf16[2,768,128]{2,1,0:T(8,128)(2,1)} %pad_maximum_fusion.4), channel_id=1, source_target_pairs={{0,2},{1,3},{2,4},{3,5},{4,6},{5,7},{6,8},{7,9},{8,10},{9,11},{10,... | collective-permute-start | bytes 1179656 | tf_op jit(solution)/shard_map/ppermute | solution.py:12
  9.3 61.5 %collective-permute-start.2 = (bf16[2,768,128]{2,1,0:T(8,128)(2,1)}, bf16[2,768,128]{2,1,0:T(8,128)(2,1)}, u32[]{:S(2)}, u32[]{:S(2)}) collective-permute-start(bf16[2,768,128]{2,1,0:T(8,128)(2,1)} %pad_maximum_fusion.4), channel_id=1, source_target_pairs={{0,3},{1,4},{2,5},{3,6},{4,7},{5,8},{6,9},{7,10},{8,11},{9,12},{10... | collective-permute-start | bytes 1179656 | tf_op jit(solution)/shard_map/ppermute | solution.py:12
  33.7 0.7 copy-start.4
  40.0 4.3 %slice-start = ((s8[4718592]{0:T(1024)(128)(4,1)}), s8[524288]{0:T(1024)(128)(4,1)S(1)}, s32[]{:S(2)}) async-start(s8[4718592]{0:T(1024)(128)(4,1)} %bitcast.93), calls=%async_computation | async-start | bytes 1048576 | tf_op jit(solution)/shard_map/cond
  40.1 4.2 %slice-start.1 = ((s8[4718592]{0:T(1024)(128)(4,1)}), s8[4194304]{0:T(1024)(128)(4,1)S(1)}, s32[]{:S(2)}) async-start(s8[4718592]{0:T(1024)(128)(4,1)} %bitcast.93), calls=%async_computation.1 | async-start | bytes 8388608 | tf_op jit(solution)/shard_map/cond
  43.5 2.7 %copy-start.5 = (bf16[2,768,128]{2,1,0:T(8,128)(2,1)S(1)}, bf16[2,768,128]{2,1,0:T(8,128)(2,1)}, u32[]{:S(2)}) copy-start(bf16[2,768,128]{2,1,0:T(8,128)(2,1)} %get-tuple-element.59) | copy-start | bytes 1179652 | tf_op jit(solution)/shard_map/cond
  48.0 59.2 %collective-permute-start.3 = (f32[2,768,128]{2,1,0:T(8,128)}, f32[2,768,128]{2,1,0:T(8,128)}, u32[]{:S(2)}, u32[]{:S(2)}) collective-permute-start(f32[2,768,128]{2,1,0:T(8,128)} %get-tuple-element.91), channel_id=1, source_target_pairs={{1,0},{2,1},{3,2},{4,3},{5,4},{6,5},{7,6},{8,7},{9,8},{10,9},{11,1... | collective-permute-start | bytes 2359304 | tf_op jit(solution)/shard_map/ppermute | solution.py:12
  57.8 4.3 %slice-start.2 = ((s8[4718592]{0:T(1024)(128)(4,1)}), s8[524288]{0:T(1024)(128)(4,1)S(1)}, s32[]{:S(2)}) async-start(s8[4718592]{0:T(1024)(128)(4,1)} %bitcast.95), calls=%async_computation.2 | async-start | bytes 1048576 | tf_op jit(solution)/shard_map/cond
  57.9 4.2 %slice-start.3 = ((s8[4718592]{0:T(1024)(128)(4,1)}), s8[4194304]{0:T(1024)(128)(4,1)S(1)}, s32[]{:S(2)}) async-start(s8[4718592]{0:T(1024)(128)(4,1)} %bitcast.95), calls=%async_computation.3 | async-start | bytes 8388608 | tf_op jit(solution)/shard_map/cond
  66.7 53.9 %collective-permute-start.4 = (f32[2,768,128]{2,1,0:T(8,128)}, f32[2,768,128]{2,1,0:T(8,128)}, u32[]{:S(2)}, u32[]{:S(2)}) collective-permute-start(f32[2,768,128]{2,1,0:T(8,128)} %get-tuple-element.92), channel_id=1, source_target_pairs={{2,0},{3,1},{4,2},{5,3},{6,4},{7,5},{8,6},{9,7},{10,8},{11,9},{12,... | collective-permute-start | bytes 2359304 | tf_op jit(solution)/shard_map/ppermute | solution.py:12
  72.7 69.2 %collective-permute-start.5 = (f32[2,768,128]{2,1,0:T(8,128)}, f32[2,768,128]{2,1,0:T(8,128)}, u32[]{:S(2)}, u32[]{:S(2)}) collective-permute-start(f32[2,768,128]{2,1,0:T(8,128)} %get-tuple-element.93), channel_id=1, source_target_pairs={{3,0},{4,1},{5,2},{6,3},{7,4},{8,5},{9,6},{10,7},{11,8},{12,9},{13... | collective-permute-start | bytes 2359304 | tf_op jit(solution)/shard_map/ppermute | solution.py:12
  91.2 6.4 %copy-start.3 = (bf16[768,128]{1,0:T(8,128)(2,1)S(1)}, bf16[768,128]{1,0:T(8,128)(2,1)}, u32[]{:S(2)}) copy-start(bf16[768,128]{1,0:T(8,128)(2,1)} %get-tuple-element.55) | copy-start | bytes 589828 | tf_op jit(solution)/shard_map/cond
  97.6 4.2 %slice-start.6 = ((s8[4718592]{0:T(1024)(128)(4,1)}), s8[4194304]{0:T(1024)(128)(4,1)S(1)}, s32[]{:S(2)}) async-start(s8[4718592]{0:T(1024)(128)(4,1)} %bitcast.99), calls=%async_computation.6 | async-start | bytes 8388608 | tf_op jit(solution)/shard_map/cond
  97.6 4.1 %slice-start.7 = ((s8[4718592]{0:T(1024)(128)(4,1)}), s8[524288]{0:T(1024)(128)(4,1)S(1)}, s32[]{:S(2)}) async-start(s8[4718592]{0:T(1024)(128)(4,1)} %bitcast.99), calls=%async_computation.7 | async-start | bytes 1048576 | tf_op jit(solution)/shard_map/cond
  100.9 2.6 %copy-start.2 = (bf16[768,128]{1,0:T(8,128)(2,1)S(1)}, bf16[768,128]{1,0:T(8,128)(2,1)}, u32[]{:S(2)}) copy-start(bf16[768,128]{1,0:T(8,128)(2,1)} %get-tuple-element.52) | copy-start | bytes 589828 | tf_op jit(solution)/shard_map/cond
where the time goes:
time: 146 us; the launch traced here: 145 us
  waiting for transfers between devices  47.2 us (32%)
  starting transfers between devices  35.6 us (24%)
  matrix products  31.5 us (22%)
  other arithmetic  15.8 us (11%)
  local copies, waits for them, and re-layouts  10.4 us (7%)
  between operations  3.52 us (2%)
    ppermute x6, waiting for transfers between devices, passed_along(): lax.ppermute(value, axis, [(source, source + steps) for source in range(l...  47.2 us
    ppermute x6, starting transfers between devices, passed_along(): lax.ppermute(value, axis, [(source, source + steps) for source in range(l...  35.6 us
    dot_general x3, matrix products, compute(): lax.dot_general(query_flat, own_block[0], contract_last, preferred_elemen...  13.3 us
    dot_general x3, matrix products, compute(): lax.dot_general(grad_flat, own_block[1], contract_last, preferred_element...  10 us
    dot_general x3, matrix products, compute(): jnp.dot(score_half, own_block[0], preferred_element_type=jnp.float32)  3.3 us
    another operation x3, other arithmetic, compute(): jnp.stack([grad_key, grad_value])  3 us
    another operation x6, local copies, waits for them, and re-layouts  2.97 us
  transfers between devices with their start and end apart: 6, of which 3 were waited for; matrix products, arithmetic and copies ran while one was open for 36% of the time, Pallas kernels for 0%

commit v1 on v0

v1 whole, which is shorter than its diff:
```python
import functools

import jax
import jax.numpy as jnp
from jax import lax
from jax.experimental import pallas as pl
from jax.experimental.pallas import tpu as pltpu
from jax.sharding import PartitionSpec as P

AXES = ("cpx", "cpy")
HEAD_DIM = 128
SCALE = HEAD_DIM**-0.5
LOG2E = 1.4426950408889634
KEY_TILE = 128
ROW_TILE = 512
LAST_BY_LAST = (((1,), (1,)), ((), ()))
FIRST_BY_FIRST = (((0,), (0,)), ((), ()))
F32, BF16, I32 = jnp.float32, jnp.bfloat16, jnp.int32


def passed_along(value, steps):
    count = lax.axis_size(AXES)
    return lax.ppermute(value, AXES, [(d, (d + steps) % count) for d in range(count)])


def make_weights(distance, k_ref, v_ref, q_ref, g_ref, stats_ref, w_ref, s_ref):
    block, flat = w_ref.shape
    rows = flat // 8

    def columns(j, carry):
        cs = pl.ds(pl.multiple_of(j * ROW_TILE, ROW_TILE), ROW_TILE)
        q, g = q_ref[cs, :], g_ref[cs, :]
        lse, delta = stats_ref[0:1, cs], stats_ref[1:2, cs]
        first_key = stats_ref[2:3, cs] + float(distance * block)
        for i in range(block // KEY_TILE):
            ks = slice(i * KEY_TILE, (i + 1) * KEY_TILE)
            scores = lax.dot_general(k_ref[ks, :], q, LAST_BY_LAST, preferred_element_type=F32)
            grad_w = lax.dot_general(v_ref[ks, :], g, LAST_BY_LAST, preferred_element_type=F32)
            key = (lax.broadcasted_iota(I32, (KEY_TILE, ROW_TILE), 0) + i * KEY_TILE).astype(F32)
            allowed = key >= first_key
            if distance == 0 and (i + 1) * KEY_TILE > block - rows:
                allowed = allowed & (key <= stats_ref[3:4, cs])
            weights = jnp.where(allowed, jnp.exp2(scores * (SCALE * LOG2E) - lse), 0.0)
            w_ref[ks, cs] = weights.astype(BF16)
            s_ref[ks, cs] = (weights * (grad_w - delta)).astype(BF16)
        return carry

    lax.fori_loop(0, flat // ROW_TILE, columns, 0)


def key_value_grads(q_ref, g_ref, w_ref, s_ref, dk_ref, dv_ref):
    dk = jnp.dot(s_ref[...], q_ref[...], preferred_element_type=F32) * SCALE
    dk_ref[...] = dk.astype(dk_ref.dtype)
    dv_ref[...] = jnp.dot(w_ref[...], g_ref[...], preferred_element_type=F32).astype(dv_ref.dtype)


def query_grads(k_ref, s_ref):
    return lax.dot_general(k_ref[...], s_ref[...], FIRST_BY_FIRST, preferred_element_type=F32) * SCALE


def own_kernel(
    lens_hbm, steps_hbm, q_hbm, g_hbm, o_hbm, lse_hbm, k_hbm, v_hbm,
    q_ref, g_ref, stats_ref, flags_ref, dk_ref, dv_ref, dq_ref,
    o_ref, w_ref, s_ref, lse_ref, k_ref, v_ref, lens_ref, steps_ref, head_sems, sems,
):
    rows = q_hbm.shape[0]
    block, head_dim = k_hbm.shape
    heads = q_hbm.shape[1] // head_dim
    flat = rows * heads
    device = lax.axis_index(AXES)
    whole = [
        pltpu.make_async_copy(source, target, sems.at[i])
        for i, (source, target) in enumerate(
            [
                (lens_hbm, lens_ref),
                (steps_hbm, steps_ref),
                (lse_hbm, lse_ref),
                (k_hbm, k_ref),
                (v_hbm, v_ref),
            ]
        )
    ]
    by_head = [
        pltpu.make_async_copy(
            source.at[:, h * head_dim : (h + 1) * head_dim],
            target.at[h * rows : (h + 1) * rows, :],
            head_sems.at[i, h],
        )
        for i, (source, target) in enumerate([(g_hbm, g_ref), (o_hbm, o_ref), (q_hbm, q_ref)])
        for h in range(heads)
    ]
    for copy in whole + by_head:
        copy.start()
    for copy in whole + by_head:
        copy.wait()
    for h in range(heads):
        stats_ref[0:1, h * rows : (h + 1) * rows] = lse_ref[h : h + 1, :] * LOG2E
    for c in range(flat // 128):
        cs = slice(c * 128, (c + 1) * 128)
        product = g_ref[cs, :].astype(F32) * o_ref[cs, :].astype(F32)
        stats_ref[1:2, cs] = jnp.sum(product.T, axis=0, keepdims=True)
    column = lax.broadcasted_iota(I32, (1, flat), 1)
    head = jnp.zeros((1, flat), I32)
    for h in range(1, heads):
        head = head + (column >= h * rows).astype(I32)
    local = column - head * rows + (block - rows)
    base = device * block
    query_pos = local + base

    def one_end(i, carry):
        end, starts, first = carry
        end = end + lens_ref[i]
        starts = jnp.where(query_pos >= end, end, starts)
        first = jnp.where(base + (block - rows) >= end, end, first)
        return end, starts, first

    zero = jnp.int32(0)
    _, starts, first = lax.fori_loop(
        0, lens_ref.shape[0], one_end, (zero, jnp.zeros((1, flat), I32), zero)
    )
    stats_ref[2:3, :] = (starts - base).astype(F32)
    stats_ref[3:4, :] = local.astype(F32)
    for t in range(steps_ref.shape[0]):
        owner = device - t
        active = (owner >= 0) & (steps_ref[t, device] == owner) & (first < (owner + 1) * block)
        flags_ref[t] = active.astype(I32)

    @pl.when(flags_ref[0] == 1)
    def _():
        make_weights(0, k_ref, v_ref, q_ref, g_ref, stats_ref, w_ref, s_ref)
        key_value_grads(q_ref, g_ref, w_ref, s_ref, dk_ref, dv_ref)
        dq_ref[...] = query_grads(k_ref, s_ref)

    @pl.when(flags_ref[0] == 0)
    def _():
        dk_ref[...] = jnp.zeros_like(dk_ref)
        dv_ref[...] = jnp.zeros_like(dv_ref)
        dq_ref[...] = jnp.zeros_like(dq_ref)


def block_kernel(
    distance, flags_ref, stats_ref, q_ref, g_ref, k_ref, v_ref, dq_in,
    dk_ref, dv_ref, dq_ref, w_ref, s_ref,
):
    @pl.when(flags_ref[distance] == 1)
    def _():
        make_weights(distance, k_ref, v_ref, q_ref, g_ref, stats_ref, w_ref, s_ref)
        key_value_grads(q_ref, g_ref, w_ref, s_ref, dk_ref, dv_ref)
        dq_ref[...] = dq_in[...] + query_grads(k_ref, s_ref)

    @pl.when(flags_ref[distance] == 0)
    def _():
        dk_ref[...] = jnp.zeros_like(dk_ref)
        dv_ref[...] = jnp.zeros_like(dv_ref)
        dq_ref[...] = dq_in[...]


def last_block_kernel(
    distance, flags_ref, stats_ref, q_ref, g_ref, k_ref, v_ref, dk_ref, dv_ref, s_ref, w_ref
):
    @pl.when(flags_ref[distance] == 1)
    def _():
        make_weights(distance, k_ref, v_ref, q_ref, g_ref, stats_ref, w_ref, s_ref)
        key_value_grads(q_ref, g_ref, w_ref, s_ref, dk_ref, dv_ref)

    @pl.when(flags_ref[distance] == 0)
    def _():
        dk_ref[...] = jnp.zeros_like(dk_ref)
        dv_ref[...] = jnp.zeros_like(dv_ref)


def queries_kernel(distance, flags_ref, k_ref, s_ref, dq_in, out_ref, dq_ref):
    rows, width = out_ref.shape
    head_dim = k_ref.shape[1]
    dq_ref[...] = dq_in[...]

    @pl.when(flags_ref[distance] == 1)
    def _():
        dq_ref[...] += query_grads(k_ref, s_ref)

    by_row = dq_ref[...].T
    for h in range(width // head_dim):
        out_ref[:, h * head_dim : (h + 1) * head_dim] = by_row[h * rows : (h + 1) * rows, :]


def call(kernel, name, outs, scratch, args, places=None, smem_outs=(), aliases=None, limit=40):
    vmem, smem = pl.BlockSpec(memory_space=pltpu.VMEM), pl.BlockSpec(memory_space=pltpu.SMEM)
    if places is None:
        places = [smem] + [vmem] * (len(args) - 1)
    return pl.pallas_call(
        kernel,
        name=name,
        out_shape=[jax.ShapeDtypeStruct(s, d) for s, d in outs],
        in_specs=places,
        out_specs=[smem if i in smem_outs else vmem for i in range(len(outs))],
        scratch_shapes=scratch,
        input_output_aliases=aliases or {},
        cost_estimate=pl.CostEstimate(flops=0, bytes_accessed=0, transcendentals=0),
        compiler_params=pltpu.CompilerParams(vmem_limit_bytes=limit << 20),
    )(*args)


def local(queries, grad_out, attn_out, saved_lse, key_rows, value_rows, doc_lengths, read_steps):
    rows, width = queries.shape
    block, head_dim = key_rows.shape
    heads = width // head_dim
    flat = rows * heads
    half = ((block, head_dim), BF16)
    full = ((block, head_dim), F32)
    scores = ((block, flat), BF16)
    flat_rows = ((flat, head_dim), BF16)
    total = ((head_dim, flat), F32)
    scores_scratch = pltpu.VMEM(*scores)
    own = (doc_lengths, read_steps.T, queries, grad_out, attn_out, saved_lse, key_rows, value_rows)

    k1 = passed_along(key_rows, 1)
    v3 = passed_along(value_rows, 3)
    v1 = passed_along(value_rows, 1)
    k3 = passed_along(key_rows, 3)
    q, g, stats, flags, dk0, dv0, dq = call(
        own_kernel, "own_block",
        [flat_rows, flat_rows, ((8, flat), F32), ((8,), I32), full, full, total],
        [
            pltpu.VMEM(*flat_rows), scores_scratch, scores_scratch, pltpu.VMEM((heads, rows), F32),
            pltpu.VMEM(*half), pltpu.VMEM(*half),
            pltpu.SMEM(own[0].shape, I32), pltpu.SMEM(own[1].shape, I32),
            pltpu.SemaphoreType.DMA((3, heads)), pltpu.SemaphoreType.DMA((5,)),
        ],
        own, [pl.BlockSpec(memory_space=pltpu.HBM)] * 8, smem_outs=(3,), limit=54,
    )
    k1, v3, flags = lax.optimization_barrier((k1, v3, flags))
    k2 = passed_along(k1, 1)
    v2 = passed_along(v3, -1)

    def other(distance, k, v, dq, outs):
        return call(
            functools.partial(block_kernel, distance), f"block_{distance}",
            [*outs, total], [scores_scratch] * 2, (flags, stats, q, g, k, v, dq),
        )

    dk1, dv1, dq = other(1, k1, v1, dq, [full, half])
    dv1 = passed_along(dv1, -1)
    dk3, dv3, dq = other(3, k3, v3, dq, [half, full])
    dk3 = passed_along(dk3, -3)
    k2, v2, dq = lax.optimization_barrier((k2, v2, dq))
    dk2, dv2, s2 = call(
        functools.partial(last_block_kernel, 2), "block_2",
        [half, half, scores], [scores_scratch], (flags, stats, q, g, k2, v2),
    )
    dk2 = passed_along(dk2, -1)
    dv2 = passed_along(dv2, 1)
    dv1, dk3, dq = lax.optimization_barrier((dv1, dk3, dq))
    (grad_queries,) = call(
        functools.partial(queries_kernel, 2), "queries",
        [((rows, width), F32)], [pltpu.VMEM(*total)], (flags, k2, s2, dq),
    )
    dk1 = passed_along((dk1 + dk2.astype(F32)).astype(BF16), -1)
    dv3 = passed_along((dv3 + dv2.astype(F32)).astype(BF16), -3)
    grad_keys = dk0 + dk3.astype(F32) + dk1.astype(F32)
    grad_values = dv0 + dv1.astype(F32) + dv3.astype(F32)
    return grad_queries, grad_keys, grad_values


def solution(mesh):
    return jax.shard_map(
        local,
        mesh=mesh,
        in_specs=(
            P(AXES, None),
            P(AXES, None),
            P(AXES, None),
            P(None, AXES),
            P(AXES, None),
            P(AXES, None),
            P(),
            P(),
        ),
        out_specs=(P(AXES, None), P(AXES, None), P(AXES, None)),
        check_vma=False,
    )
```

time: 146 us -> 80.3 us (0.55)
  the two profiles are of different devices: /device:TPU:173 before, /device:TPU:1 now
where the time goes in v1:
time: 80.3 us; the launch traced here: 79.8 us
  waiting for transfers between devices  29.2 us (36%)
  starting transfers between devices  28.5 us (35%)
  Pallas kernels  15.1 us (19%)
  local copies, waits for them, and re-layouts  4.56 us (6%)
  other arithmetic  1.7 us (2%)
    ppermute x12, waiting for transfers between devices, passed_along(): lax.ppermute(value, AXES, [(d, (d + steps) % count) for d in range(count)])  29.2 us
    ppermute x12, starting transfers between devices, passed_along(): lax.ppermute(value, AXES, [(d, (d + steps) % count) for d in range(count)])  28.5 us
    pallas_call x5, Pallas kernels, call(): pl.pallas_call(kernel, name=name, out_shape=[jax.ShapeDtypeStruct(s, d) f...  15.1 us
    unnamed x14, local copies, waits for them, and re-layouts  4.56 us
  transfers between devices with their start and end apart: 12, of which 7 were waited for; matrix products, arithmetic and copies ran while one was open for 1% of the time, Pallas kernels for 19%

profile of v1, /device:TPU:1, one launch (start us, length us, event | category | flops | bytes accessed | tf_op | source)
XLA Modules:
  0.0 79.8 jit_solution(8924499717538054388)
XLA Ops:
  0.6 3.9 %collective-permute-start = (bf16[768,128]{1,0:T(8,128)(2,1)}, bf16[768,128]{1,0:T(8,128)(2,1)S(1)}, u32[]{:S(2)}, u32[]{:S(2)}) collective-permute-start(bf16[768,128]{1,0:T(8,128)(2,1)} %k_hbm.1), channel_id=1, source_target_pairs={{0,1},{1,2},{2,3},{3,4},{4,5},{5,6},{6,7},{7,8},{8,9},{9,10},{10,1... | collective-permute-start | bytes 589832 | tf_op jit(solution)/shard_map/ppermute | solution.py:23
  4.5 3.1 %collective-permute-start.1 = (bf16[768,128]{1,0:T(8,128)(2,1)}, bf16[768,128]{1,0:T(8,128)(2,1)S(1)}, u32[]{:S(2)}, u32[]{:S(2)}) collective-permute-start(bf16[768,128]{1,0:T(8,128)(2,1)} %v_hbm.1), channel_id=1, source_target_pairs={{0,3},{1,4},{2,5},{3,6},{4,7},{5,8},{6,9},{7,10},{8,11},{9,12},{10... | collective-permute-start | bytes 589832 | tf_op jit(solution)/shard_map/ppermute | solution.py:23
  7.7 3.2 %collective-permute-start.4 = (bf16[768,128]{1,0:T(8,128)(2,1)}, bf16[768,128]{1,0:T(8,128)(2,1)S(1)}, u32[]{:S(2)}, u32[]{:S(2)}) collective-permute-start(bf16[768,128]{1,0:T(8,128)(2,1)} %k_hbm.1), channel_id=1, source_target_pairs={{0,3},{1,4},{2,5},{3,6},{4,7},{5,8},{6,9},{7,10},{8,11},{9,12},{10... | collective-permute-start | bytes 589832 | tf_op jit(solution)/shard_map/ppermute | solution.py:23
  10.9 0.1 collective-permute-start.5
  10.9 7.7 %own_block.1 = (bf16[1536,128]{1,0:T(8,128)(2,1)}, bf16[1536,128]{1,0:T(8,128)(2,1)}, f32[8,1536]{1,0:T(8,128)}, s32[8]{0:T(128)}, f32[768,128]{1,0:T(8,128)}, /*index=5*/f32[768,128]{1,0:T(8,128)}, f32[128,1536]{1,0:T(8,128)}) custom-call(s32[64]{0:T(128)} %lens_hbm.1, s32[4,256]{1,0:T(4,128)} %bitcast.1, bf16[192,1024]{1,0:T(8,128)(2,1)} %q_hbm.1, ...), custom_call_target="tpu_custom_call" | custom-call | tf_op jit(solution)/shard_map/own_block/pallas_call | solution.py:190
  18.7 0.0 collective-permute-done.k_ref
  18.7 7.2 %collective-permute-done.1.v_ref = bf16[768,128]{1,0:T(8,128)(2,1)S(1)} collective-permute-done((bf16[768,128]{1,0:T(8,128)(2,1)}, bf16[768,128]{1,0:T(8,128)(2,1)S(1)}, u32[]{:S(2)}, u32[]{:S(2)}) %collective-permute-start.1) | collective-permute-done | bytes 196640 | tf_op jit(solution)/shard_map/ppermute | solution.py:23
  26.0 0.0 collective-permute-start.2
  26.0 6.0 %collective-permute-start.3 = (bf16[768,128]{1,0:T(8,128)(2,1)S(1)}, bf16[768,128]{1,0:T(8,128)(2,1)S(1)}, u32[]{:S(2)}, u32[]{:S(2)}) collective-permute-start(bf16[768,128]{1,0:T(8,128)(2,1)S(1)} %collective-permute-done.1.v_ref), channel_id=1, source_target_pairs={{0,255},{1,0},{2,1},{3,2},{4,3},{5,4},{6,5},{7,6},{8,7},{9,8},{10,... | collective-permute-start | bytes 589832 | tf_op jit(solution)/shard_map/ppermute | solution.py:23
  31.9 0.0 collective-permute-done.5.v_ref
  31.9 0.0 copy-start
  31.9 1.0 %copy-done = bf16[1536,128]{1,0:T(8,128)(2,1)S(1)} copy-done((bf16[1536,128]{1,0:T(8,128)(2,1)S(1)}, bf16[1536,128]{1,0:T(8,128)(2,1)}, u32[]{:S(2)}) %copy-start) | copy-done | bytes 393240
  32.9 0.0 copy-start.1
  32.9 1.0 %copy-done.1 = bf16[1536,128]{1,0:T(8,128)(2,1)S(1)} copy-done((bf16[1536,128]{1,0:T(8,128)(2,1)S(1)}, bf16[1536,128]{1,0:T(8,128)(2,1)}, u32[]{:S(2)}) %copy-start.1) | copy-done | bytes 393240
  33.9 0.0 copy-start.2
  33.9 1.1 %copy-done.2 = f32[128,1536]{1,0:T(8,128)S(1)} copy-done((f32[128,1536]{1,0:T(8,128)S(1)}, f32[128,1536]{1,0:T(8,128)}, u32[]{:S(2)}) %copy-start.2) | copy-done | bytes 786456
  35.1 0.0 copy-start.3
  35.1 0.8 copy-done.3
  35.9 0.0 copy-start.4
  35.9 0.6 copy-done.4
  36.5 0.7 block_1.1
  37.1 0.0 collective-permute-done.4.k_ref
  37.2 0.7 block_3.1
  37.8 5.5 %collective-permute-start.7 = (bf16[768,128]{1,0:T(8,128)(2,1)S(1)}, bf16[768,128]{1,0:T(8,128)(2,1)S(1)}, u32[]{:S(2)}, u32[]{:S(2)}) collective-permute-start(bf16[768,128]{1,0:T(8,128)(2,1)S(1)} %get-tuple-element.42), channel_id=1, source_target_pairs={{0,253},{1,254},{2,255},{3,0},{4,1},{5,2},{6,3},{7,4},{8,5},{9,6},... | collective-permute-start | bytes 589832 | tf_op jit(solution)/shard_map/ppermute | solution.py:23
  43.4 1.7 %collective-permute-start.6 = (bf16[768,128]{1,0:T(8,128)(2,1)S(1)}, bf16[768,128]{1,0:T(8,128)(2,1)S(1)}, u32[]{:S(2)}, u32[]{:S(2)}) collective-permute-start(bf16[768,128]{1,0:T(8,128)(2,1)S(1)} %get-tuple-element.41), channel_id=1, source_target_pairs={{0,255},{1,0},{2,1},{3,2},{4,3},{5,4},{6,5},{7,6},{8,7},{9,8},{10,... | collective-permute-start | bytes 589832 | tf_op jit(solution)/shard_map/ppermute | solution.py:23
  45.1 0.0 collective-permute-done.2.k_ref
  45.1 0.0 collective-permute-done.3.v_ref
  45.1 3.8 %block_2.1 = (bf16[768,128]{1,0:T(8,128)(2,1)S(1)}, bf16[768,128]{1,0:T(8,128)(2,1)S(1)}, bf16[768,1536]{1,0:T(8,128)(2,1)S(1)}) custom-call(s32[8]{0:T(128)S(1)} %copy-done.4, f32[8,1536]{1,0:T(8,128)S(1)} %copy-done.3, bf16[1536,128]{1,0:T(8,128)(2,1)S(1)} %copy-done, bf16[1536,128]{1,0:T(8,128)(2,1)S(1)} %copy-done.1, ...), custom_call_target="tpu_custom_call" | custom-call | tf_op jit(solution)/shard_map/block_2/pallas_call | solution.py:190
  48.9 0.1 collective-permute-start.8
  49.0 2.6 %collective-permute-done.7 = bf16[768,128]{1,0:T(8,128)(2,1)S(1)} collective-permute-done((bf16[768,128]{1,0:T(8,128)(2,1)S(1)}, bf16[768,128]{1,0:T(8,128)(2,1)S(1)}, u32[]{:S(2)}, u32[]{:S(2)}) %collective-permute-start.7) | collective-permute-done | bytes 196640 | tf_op jit(solution)/shard_map/ppermute | solution.py:23
  51.6 7.6 %collective-permute-done.6 = bf16[768,128]{1,0:T(8,128)(2,1)S(1)} collective-permute-done((bf16[768,128]{1,0:T(8,128)(2,1)S(1)}, bf16[768,128]{1,0:T(8,128)(2,1)S(1)}, u32[]{:S(2)}, u32[]{:S(2)}) %collective-permute-start.6) | collective-permute-done | bytes 196640 | tf_op jit(solution)/shard_map/ppermute | solution.py:23
  59.1 1.8 %collective-permute-start.10 = (bf16[768,128]{1,0:T(8,128)(2,1)S(1)}, bf16[768,128]{1,0:T(8,128)(2,1)S(1)}, u32[]{:S(2)}, u32[]{:S(2)}) collective-permute-start(bf16[768,128]{1,0:T(8,128)(2,1)S(1)} %get-tuple-element.52), channel_id=1, source_target_pairs={{0,1},{1,2},{2,3},{3,4},{4,5},{5,6},{6,7},{7,8},{8,9},{9,10},{10,1... | collective-permute-start | bytes 589832 | tf_op jit(solution)/shard_map/ppermute | solution.py:23
  61.0 0.0 copy-start.6
  61.0 2.3 %queries.1 = f32[192,1024]{1,0:T(8,128)} custom-call(s32[8]{0:T(128)S(1)} %copy-done.4, bf16[768,128]{1,0:T(8,128)(2,1)S(1)} %collective-permute-done.2.k_ref, bf16[768,1536]{1,0:T(8,128)(2,1)S(1)} %get-tuple-element.40.s_ref, f32[128,1536]{1,0:T(8,128)S(1)} %get-tuple-element.44.dq_in), custom_call_target="tpu_custom_call" | custom-call | tf_op jit(solution)/shard_map/queries/pallas_call | solution.py:190
  63.2 0.0 copy-start.5
  63.2 0.7 collective-permute-done.8
  64.0 3.0 %collective-permute-start.9 = (bf16[768,128]{1,0:T(8,128)(2,1)S(1)}, bf16[768,128]{1,0:T(8,128)(2,1)S(1)}, u32[]{:S(2)}, u32[]{:S(2)}) collective-permute-start(bf16[768,128]{1,0:T(8,128)(2,1)S(1)} %add_convert_fusion.1), channel_id=1, source_target_pairs={{0,255},{1,0},{2,1},{3,2},{4,3},{5,4},{6,5},{7,6},{8,7},{9,8},{10,... | collective-permute-start | bytes 589832 | tf_op jit(solution)/shard_map/ppermute | solution.py:23
  67.0 2.7 %collective-permute-done.10 = bf16[768,128]{1,0:T(8,128)(2,1)S(1)} collective-permute-done((bf16[768,128]{1,0:T(8,128)(2,1)S(1)}, bf16[768,128]{1,0:T(8,128)(2,1)S(1)}, u32[]{:S(2)}, u32[]{:S(2)}) %collective-permute-start.10) | collective-permute-done | bytes 196640 | tf_op jit(solution)/shard_map/ppermute | solution.py:23
  69.7 0.1 add_convert_fusion
  69.8 0.1 collective-permute-start.11
  69.9 3.8 %collective-permute-done.9 = bf16[768,128]{1,0:T(8,128)(2,1)S(1)} collective-permute-done((bf16[768,128]{1,0:T(8,128)(2,1)S(1)}, bf16[768,128]{1,0:T(8,128)(2,1)S(1)}, u32[]{:S(2)}, u32[]{:S(2)}) %collective-permute-start.9) | collective-permute-done | bytes 196640 | tf_op jit(solution)/shard_map/ppermute | solution.py:23
  73.6 0.0 copy-done.6
  73.6 0.8 %convert_add_fusion.1 = f32[768,128]{1,0:T(8,128)} fusion(bf16[768,128]{1,0:T(8,128)(2,1)S(1)} %collective-permute-done.9, f32[768,128]{1,0:T(8,128)S(1)} %copy-done.6, bf16[768,128]{1,0:T(8,128)(2,1)S(1)} %collective-permute-done.7), kind=kLoop, calls=%fused_computation.2 | loop fusion | flops 393216 | bytes 1179648 | tf_op jit(solution)/shard_map/add | solution.py:259
  74.4 4.5 %collective-permute-done.11 = bf16[768,128]{1,0:T(8,128)(2,1)S(1)} collective-permute-done((bf16[768,128]{1,0:T(8,128)(2,1)S(1)}, bf16[768,128]{1,0:T(8,128)(2,1)S(1)}, u32[]{:S(2)}, u32[]{:S(2)}) %collective-permute-start.11) | collective-permute-done | bytes 196640 | tf_op jit(solution)/shard_map/ppermute | solution.py:23
  79.0 0.0 copy-done.5
  79.0 0.8 %convert_add_fusion = f32[768,128]{1,0:T(8,128)} fusion(bf16[768,128]{1,0:T(8,128)(2,1)S(1)} %collective-permute-done.11, f32[768,128]{1,0:T(8,128)S(1)} %copy-done.5, bf16[768,128]{1,0:T(8,128)(2,1)S(1)} %collective-permute-done.6), kind=kLoop, calls=%fused_computation | loop fusion | flops 393216 | bytes 1179648 | tf_op jit(solution)/shard_map/add | solution.py:260
  (1 shorter events, 0.0 us)
Async XLA Ops:
  0.6 18.1 %collective-permute-start = (bf16[768,128]{1,0:T(8,128)(2,1)}, bf16[768,128]{1,0:T(8,128)(2,1)S(1)}, u32[]{:S(2)}, u32[]{:S(2)}) collective-permute-start(bf16[768,128]{1,0:T(8,128)(2,1)} %k_hbm.1), channel_id=1, source_target_pairs={{0,1},{1,2},{2,3},{3,4},{4,5},{5,6},{6,7},{7,8},{8,9},{9,10},{10,1... | collective-permute-start | bytes 589832 | tf_op jit(solution)/shard_map/ppermute | solution.py:23
  4.5 21.4 %collective-permute-start.1 = (bf16[768,128]{1,0:T(8,128)(2,1)}, bf16[768,128]{1,0:T(8,128)(2,1)S(1)}, u32[]{:S(2)}, u32[]{:S(2)}) collective-permute-start(bf16[768,128]{1,0:T(8,128)(2,1)} %v_hbm.1), channel_id=1, source_target_pairs={{0,3},{1,4},{2,5},{3,6},{4,7},{5,8},{6,9},{7,10},{8,11},{9,12},{10... | collective-permute-start | bytes 589832 | tf_op jit(solution)/shard_map/ppermute | solution.py:23
  7.7 29.5 %collective-permute-start.4 = (bf16[768,128]{1,0:T(8,128)(2,1)}, bf16[768,128]{1,0:T(8,128)(2,1)S(1)}, u32[]{:S(2)}, u32[]{:S(2)}) collective-permute-start(bf16[768,128]{1,0:T(8,128)(2,1)} %k_hbm.1), channel_id=1, source_target_pairs={{0,3},{1,4},{2,5},{3,6},{4,7},{5,8},{6,9},{7,10},{8,11},{9,12},{10... | collective-permute-start | bytes 589832 | tf_op jit(solution)/shard_map/ppermute | solution.py:23
  10.9 21.1 %collective-permute-start.5 = (bf16[768,128]{1,0:T(8,128)(2,1)}, bf16[768,128]{1,0:T(8,128)(2,1)S(1)}, u32[]{:S(2)}, u32[]{:S(2)}) collective-permute-start(bf16[768,128]{1,0:T(8,128)(2,1)} %v_hbm.1), channel_id=1, source_target_pairs={{0,1},{1,2},{2,3},{3,4},{4,5},{5,6},{6,7},{7,8},{8,9},{9,10},{10,1... | collective-permute-start | bytes 589832 | tf_op jit(solution)/shard_map/ppermute | solution.py:23
  26.0 19.1 %collective-permute-start.2 = (bf16[768,128]{1,0:T(8,128)(2,1)S(1)}, bf16[768,128]{1,0:T(8,128)(2,1)S(1)}, u32[]{:S(2)}, u32[]{:S(2)}) collective-permute-start(bf16[768,128]{1,0:T(8,128)(2,1)S(1)} %collective-permute-done.k_ref), channel_id=1, source_target_pairs={{0,1},{1,2},{2,3},{3,4},{4,5},{5,6},{6,7},{7,8},{8,9},{9,10},{10,1... | collective-permute-start | bytes 589832 | tf_op jit(solution)/shard_map/ppermute | solution.py:23
  26.0 19.1 %collective-permute-start.3 = (bf16[768,128]{1,0:T(8,128)(2,1)S(1)}, bf16[768,128]{1,0:T(8,128)(2,1)S(1)}, u32[]{:S(2)}, u32[]{:S(2)}) collective-permute-start(bf16[768,128]{1,0:T(8,128)(2,1)S(1)} %collective-permute-done.1.v_ref), channel_id=1, source_target_pairs={{0,255},{1,0},{2,1},{3,2},{4,3},{5,4},{6,5},{7,6},{8,7},{9,8},{10,... | collective-permute-start | bytes 589832 | tf_op jit(solution)/shard_map/ppermute | solution.py:23
  31.9 1.0 %copy-start = (bf16[1536,128]{1,0:T(8,128)(2,1)S(1)}, bf16[1536,128]{1,0:T(8,128)(2,1)}, u32[]{:S(2)}) copy-start(bf16[1536,128]{1,0:T(8,128)(2,1)} %get-tuple-element.33.q_ref) | copy-start | bytes 1179652
  32.9 1.0 %copy-start.1 = (bf16[1536,128]{1,0:T(8,128)(2,1)S(1)}, bf16[1536,128]{1,0:T(8,128)(2,1)}, u32[]{:S(2)}) copy-start(bf16[1536,128]{1,0:T(8,128)(2,1)} %get-tuple-element.34.g_ref) | copy-start | bytes 1179652
  33.9 1.1 %copy-start.2 = (f32[128,1536]{1,0:T(8,128)S(1)}, f32[128,1536]{1,0:T(8,128)}, u32[]{:S(2)}) copy-start(f32[128,1536]{1,0:T(8,128)} %get-tuple-element.35.dq_in) | copy-start | bytes 2359300
  35.1 0.8 %copy-start.3 = (f32[8,1536]{1,0:T(8,128)S(1)}, f32[8,1536]{1,0:T(8,128)}, u32[]{:S(2)}) copy-start(f32[8,1536]{1,0:T(8,128)} %get-tuple-element.32.stats_ref) | copy-start | bytes 147460
  35.9 0.6 copy-start.4
  37.8 13.8 %collective-permute-start.7 = (bf16[768,128]{1,0:T(8,128)(2,1)S(1)}, bf16[768,128]{1,0:T(8,128)(2,1)S(1)}, u32[]{:S(2)}, u32[]{:S(2)}) collective-permute-start(bf16[768,128]{1,0:T(8,128)(2,1)S(1)} %get-tuple-element.42), channel_id=1, source_target_pairs={{0,253},{1,254},{2,255},{3,0},{4,1},{5,2},{6,3},{7,4},{8,5},{9,6},... | collective-permute-start | bytes 589832 | tf_op jit(solution)/shard_map/ppermute | solution.py:23
  43.4 15.8 %collective-permute-start.6 = (bf16[768,128]{1,0:T(8,128)(2,1)S(1)}, bf16[768,128]{1,0:T(8,128)(2,1)S(1)}, u32[]{:S(2)}, u32[]{:S(2)}) collective-permute-start(bf16[768,128]{1,0:T(8,128)(2,1)S(1)} %get-tuple-element.41), channel_id=1, source_target_pairs={{0,255},{1,0},{2,1},{3,2},{4,3},{5,4},{6,5},{7,6},{8,7},{9,8},{10,... | collective-permute-start | bytes 589832 | tf_op jit(solution)/shard_map/ppermute | solution.py:23
  48.9 15.1 %collective-permute-start.8 = (bf16[768,128]{1,0:T(8,128)(2,1)S(1)}, bf16[768,128]{1,0:T(8,128)(2,1)S(1)}, u32[]{:S(2)}, u32[]{:S(2)}) collective-permute-start(bf16[768,128]{1,0:T(8,128)(2,1)S(1)} %get-tuple-element.48), channel_id=1, source_target_pairs={{0,255},{1,0},{2,1},{3,2},{4,3},{5,4},{6,5},{7,6},{8,7},{9,8},{10,... | collective-permute-start | bytes 589832 | tf_op jit(solution)/shard_map/ppermute | solution.py:23
  59.1 10.6 %collective-permute-start.10 = (bf16[768,128]{1,0:T(8,128)(2,1)S(1)}, bf16[768,128]{1,0:T(8,128)(2,1)S(1)}, u32[]{:S(2)}, u32[]{:S(2)}) collective-permute-start(bf16[768,128]{1,0:T(8,128)(2,1)S(1)} %get-tuple-element.52), channel_id=1, source_target_pairs={{0,1},{1,2},{2,3},{3,4},{4,5},{5,6},{6,7},{7,8},{8,9},{9,10},{10,1... | collective-permute-start | bytes 589832 | tf_op jit(solution)/shard_map/ppermute | solution.py:23
  61.0 12.7 %copy-start.6 = (f32[768,128]{1,0:T(8,128)S(1)}, f32[768,128]{1,0:T(8,128)}, u32[]{:S(2)}) copy-start(f32[768,128]{1,0:T(8,128)} %get-tuple-element.45) | copy-start | bytes 1179652
  63.2 15.7 %copy-start.5 = (f32[768,128]{1,0:T(8,128)S(1)}, f32[768,128]{1,0:T(8,128)}, u32[]{:S(2)}) copy-start(f32[768,128]{1,0:T(8,128)} %get-tuple-element.49) | copy-start | bytes 1179652
  64.0 9.6 %collective-permute-start.9 = (bf16[768,128]{1,0:T(8,128)(2,1)S(1)}, bf16[768,128]{1,0:T(8,128)(2,1)S(1)}, u32[]{:S(2)}, u32[]{:S(2)}) collective-permute-start(bf16[768,128]{1,0:T(8,128)(2,1)S(1)} %add_convert_fusion.1), channel_id=1, source_target_pairs={{0,255},{1,0},{2,1},{3,2},{4,3},{5,4},{6,5},{7,6},{8,7},{9,8},{10,... | collective-permute-start | bytes 589832 | tf_op jit(solution)/shard_map/ppermute | solution.py:23
  69.8 9.2 %collective-permute-start.11 = (bf16[768,128]{1,0:T(8,128)(2,1)S(1)}, bf16[768,128]{1,0:T(8,128)(2,1)S(1)}, u32[]{:S(2)}, u32[]{:S(2)}) collective-permute-start(bf16[768,128]{1,0:T(8,128)(2,1)S(1)} %add_convert_fusion), channel_id=1, source_target_pairs={{0,253},{1,254},{2,255},{3,0},{4,1},{5,2},{6,3},{7,4},{8,5},{9,6},... | collective-permute-start | bytes 589832 | tf_op jit(solution)/shard_map/ppermute | solution.py:23
